TPU v7x, 512 devices: a whole 4x4x16 slice. The times are simulated.
512 devices in a mesh: face: 4 (over z_lo), tile: 64 (over y, z_hi, x), lev: 2 (over core).
Axes of the slice: x: 4, y: 4, z: 16 (z_hi: 4, z_lo: 4; z = z_hi * 4 + z_lo), core: 2. Of those that a mesh axis runs over, the one named last changes fastest.
Arguments:
- flux: float32 [2048, 8, 512], P(('face', 'tile')), may hold values from -6 to 6
- profile: float32 [16], P('lev'), may hold values from 0.2 to 1
- courant: float32 [2, 16, 512, 2048], P(None, 'lev', 'tile', 'face'), may hold values from 0.05 to 0.45
- winds: int32 [2, 16, 512, 2048], P(None, 'lev', 'tile', 'face'), may hold values from 0 to 1
- cells: int32 [64, 4, 128], P('tile', 'face'), may hold values from 0 to 4095, as said below
- counts: int32 [64, 4], P('tile', 'face'), may hold values from 32 to 128, as said below
- kernels: float32 [16, 64, 4, 128], P('lev', 'tile', 'face'), may hold values from 0.25 to 0.75
- month_weight: float32 [8, 64, 4, 128], P(None, 'tile', 'face'), may hold values from 0 to 1
- observed: float32 [64, 4, 128], P('tile', 'face'), may hold values from -8 to 8
- obs_weight: float32 [64, 4, 128], P('tile', 'face'), may hold values from 0.5 to 2
- precision: float32 [8], replicated, may hold values from 0.5 to 2
Outputs:
- flux_gradient: float32 [8, 512, 2048], P(None, 'tile', 'face')
- precision_gradient: float32 [8], replicated
Inputs may be any that keep to these rules, and one draw needn't show every extreme that they name: Within each block the 128 entries are distinct cells, numbered row by row over the block's 8 rows of 512 cells; the first four slots of every block hold, in some order, a cell of the block's first column, one of its last column, and interior cells of its first row and of its last row. `counts`: slot s of a block holds a sounding when s is below the block's count; some block is full and some holds exactly 32.
All inputs are finite; a program needn't handle non-finite values.
Results may differ from a plain program's by a relative error of at most 0.00015.
Values sent between devices are 32-bit elements; how exact they have to be, the bound alone decides.
A program may use at most 64 MiB of HBM per device.

v0:
```python
import jax
import jax.numpy as jnp
from jax import lax
from jax.sharding import PartitionSpec as P

KAPPA = 0.025


def extended(x, sides, width, wrap):
    for axis, dim in sides:
        devices, length = (lax.axis_size(axis), x.shape[dim])
        up = [(i, (i + 1) % devices) for i in range(devices if wrap else devices - 1)]
        down = [(j, i) for i, j in up]
        last = lax.slice_in_dim(x, length - width, length, axis=dim)
        initial = lax.slice_in_dim(x, 0, width, axis=dim)
        before = lax.ppermute(last, axis, up)
        after = lax.ppermute(initial, axis, down)
        x = jnp.concatenate([before, x, after], axis=dim)
    return x


def shifted(x, axis, by):
    devices = lax.axis_size(axis)
    return lax.ppermute(x, axis, [(i, (i + by) % devices) for i in range(devices)])


def shifted_2(value, axis, steps):
    count = lax.axis_size(axis)
    initial, last = (max(0, -steps), min(count, count - steps))
    return lax.ppermute(value, axis, [(source, source + steps) for source in range(initial, last)])


def weights_from(speed_x, speed_y, east_flag, north_flag):
    w_west = speed_x * (1.0 - east_flag) + KAPPA
    w_east = speed_x * east_flag + KAPPA
    w_south = speed_y * (1.0 - north_flag) + KAPPA
    w_north = speed_y * north_flag + KAPPA
    w_centre = 1.0 - speed_x - speed_y - 4.0 * KAPPA
    return (w_centre, w_west, w_east, w_south, w_north)


def flags_of(winds):
    return ((winds[0] == 1).astype(jnp.float32), (winds[1] == 1).astype(jnp.float32))


def advance(conc, coeffs):
    w_centre, w_west, w_east, w_south, w_north = coeffs
    side = extended(conc, (("face", 3),), 1, True)
    rim = extended(conc, (("tile", 2),), 1, False)
    return (
        w_centre * conc
        + w_west * side[..., :-2]
        + w_east * side[..., 2:]
        + w_south * rim[..., :-2, :]
        + w_north * rim[..., 2:, :]
    )


def retreat(grad, coeffs):
    w_centre, w_west, w_east, w_south, w_north = coeffs
    west_weighted = w_west * grad
    east_weighted = w_east * grad
    south_weighted = w_south * grad
    north_weighted = w_north * grad
    from_east = shifted(west_weighted[..., :1], "face", -1)
    from_west = shifted(east_weighted[..., -1:], "face", 1)
    from_above = shifted_2(south_weighted[..., :1, :], "tile", -1)
    from_below = shifted_2(north_weighted[..., -1:, :], "tile", 1)
    west_part = jnp.concatenate([west_weighted[..., 1:], from_east], -1)
    east_part = jnp.concatenate([from_west, east_weighted[..., :-1]], -1)
    south_part = jnp.concatenate([south_weighted[..., 1:, :], from_above], -2)
    north_part = jnp.concatenate([from_below, north_weighted[..., :-1, :]], -2)
    return w_centre * grad + west_part + east_part + south_part + north_part


def on_device(
    flux,
    profile,
    courant,
    winds,
    cells,
    counts,
    kernels,
    month_weight,
    observed,
    obs_weight,
    precision,
):
    n_tracer = flux.shape[1]
    n_level = profile.shape[0]
    slot_total = cells.shape[2]
    moved = lax.all_to_all(flux, "tile", split_axis=2, concat_axis=0, tiled=True)
    field = jnp.transpose(moved, (1, 2, 0))
    rows_dev = field.shape[1]
    cols_dev = field.shape[2]
    n_cell = rows_dev * cols_dev
    east_flag, north_flag = flags_of(winds)
    conc = profile[None, :, None, None] * field[:, None]
    coeffs = weights_from(courant[0], courant[1], east_flag, north_flag)
    conc = advance(advance(conc, coeffs), coeffs)
    slot_cells = cells.reshape(slot_total)
    live = jnp.arange(slot_total, dtype=jnp.int32) < counts.reshape(())
    picker = jnp.where(
        live[:, None] & (slot_cells[:, None] == jnp.arange(n_cell, dtype=jnp.int32)[None, :]),
        1.0,
        0.0,
    ).astype(jnp.float32)
    flat = conc.reshape(n_tracer, n_level, n_cell)
    sampled = jnp.einsum("tlc,sc->tls", flat, picker, precision=lax.Precision.HIGHEST)
    kern = kernels.reshape(n_level, slot_total)
    monthly = month_weight.reshape(n_tracer, slot_total)
    partial_model = jnp.sum(kern * jnp.sum(monthly[:, None, :] * sampled, 0), 0)
    model = lax.psum(partial_model, "lev")
    forcing = jnp.where(
        live, obs_weight.reshape(slot_total) * (observed.reshape(slot_total) - model), 0.0
    )
    values = kern[None] * (monthly * forcing[None])[:, None, :]
    lam = jnp.einsum("tls,sc->tlc", values, picker, precision=lax.Precision.HIGHEST)
    lam = lam.reshape(n_tracer, n_level, rows_dev, cols_dev)
    lam = retreat(retreat(lam, coeffs), coeffs)
    adj_part = jnp.sum(profile[None, :, None, None] * lam, 1)
    all_cells = n_cell * lax.axis_size("tile") * lax.axis_size("face")
    adj = lax.psum(adj_part, "lev")
    flux_gradient = precision[:, None, None] * field - adj
    square_sum = lax.psum(jnp.sum(adj * adj, axis=(1, 2)), ("face", "tile"))
    precision_gradient = 0.5 / precision - 0.5 * (square_sum / all_cells) / (precision * precision)
    return (flux_gradient, precision_gradient)


def solution(mesh):
    return jax.shard_map(
        on_device,
        mesh=mesh,
        in_specs=(
            P(("face", "tile"), None, None),
            P("lev"),
            P(None, "lev", "tile", "face"),
            P(None, "lev", "tile", "face"),
            P("tile", "face", None),
            P("tile", "face"),
            P("lev", "tile", "face", None),
            P(None, "tile", "face", None),
            P("tile", "face", None),
            P("tile", "face", None),
            P(),
        ),
        out_specs=(P(None, "tile", "face"), P()),
        check_vma=False,
    )
```

profile of v0, /device:TPU:32, one launch (start us, length us, event | category | flops | bytes accessed | tf_op | source)
XLA Modules:
  0.0 1168.7 jit_solution(5610475102505204907)
XLA Ops:
  7.2 1.7 copy.25
  8.9 1.7 reshape.69
  10.6 20.3 %all-to-all-start = ((f32[64,1,512]{2,1,0:T(1,128)}), f32[64,1,512]{2,1,0:T(1,128)S(1)}, u32[]{:S(2)}, u32[]{:S(2)}) async-start(f32[64,1,512]{2,1,0:T(1,128)} %reshape.69), calls=%async_computation | async-start | bytes 262144 | tf_op jit(solution)/shard_map/all_to_all | solution.py:92
  31.1 20.0 %all-to-all-done = f32[64,1,512]{2,1,0:T(1,128)S(1)} async-done(((f32[64,1,512]{2,1,0:T(1,128)}), f32[64,1,512]{2,1,0:T(1,128)S(1)}, u32[]{:S(2)}, u32[]{:S(2)}) %all-to-all-start) | async-done | bytes 131104 | tf_op jit(solution)/shard_map/all_to_all | solution.py:92
  51.1 0.5 broadcast.82
  51.6 0.9 reduce.1
  52.6 1.1 reshape.70
  53.7 2.4 copy.27
  56.1 2.8 all_to_all.16
  58.9 0.2 broadcast_multiply_fusion.8
  59.1 0.1 fusion.52
  59.3 2.5 collective-permute-start.2
  61.8 1.3 collective-permute-start.3
  63.1 2.9 collective-permute-start
  66.1 2.9 collective-permute-start.1
  69.7 0.1 copy.31
  69.8 0.1 copy.29
  69.9 0.1 copy.30
  70.0 0.1 copy.32
  70.0 0.1 copy.28
  70.1 4.1 collective-permute-done
  74.2 7.7 collective-permute-done.1
  81.9 0.8 fusion.24
  82.7 1.3 collective-permute-start.6
  84.0 1.3 collective-permute-start.7
  85.3 0.1 fusion.50
  85.5 5.5 collective-permute-start.4
  91.0 1.9 collective-permute-start.5
  93.0 7.6 collective-permute-done.4
  100.5 0.8 fusion.16
  101.3 2.4 fusion.12
  103.8 2.6 psum.21
  106.5 1.7 fusion
  108.2 0.6 broadcast_multiply_fusion.5
  108.8 1.3 collective-permute-start.10
  110.1 4.9 collective-permute-start.11
  115.1 0.1 slice.162
  115.2 3.2 collective-permute-start.8
  118.4 3.1 collective-permute-start.9
  121.6 0.1 copy.35
  121.7 0.1 slice.167
  121.7 0.1 slice.164
  121.8 0.3 slice.160
  122.2 3.8 collective-permute-done.8
  126.0 6.6 collective-permute-done.9
  132.5 1.1 broadcast_multiply_fusion.6
  133.6 4.2 collective-permute-start.12
  137.9 0.2 broadcast_multiply_fusion.4
  138.1 0.3 slice.168
  138.6 5.9 collective-permute-start.15
  144.5 1.3 collective-permute-start.14
  145.8 0.1 slice.170
  146.0 3.7 collective-permute-start.13
  149.7 0.2 pad_maximum_fusion.12
  149.8 7.5 collective-permute-done.13
  157.3 0.3 pad_maximum_fusion.13
  157.7 0.1 pad_maximum_fusion.15
  157.8 9.1 collective-permute-done.14
  167.0 1.1 multiply_reduce_fusion
  168.1 0.7 copy.38
  168.8 66.5 %all-reduce.2.cloned.1.call-done = f32[8,8,512]{2,1,0:T(8,128)} async-done(((f32[8,8,512]{2,1,0:T(8,128)}), f32[8,8,512]{2,1,0:T(8,128)}) %all-reduce.2.cloned.1.call-update) | async-done | bytes 131088 | tf_op jit(solution)/shard_map/psum | solution.py:123
  235.3 1.7 multiply_reduce_fusion.1
  237.0 924.4 %psum.23 = f32[8]{0:T(128)S(1)} all-reduce(f32[8]{0:T(128)S(1)} %get-tuple-element.33), channel_id=1, replica_groups=mesh['face'=4,'tile'=64,'lev'=2] {'face','tile'}, use_global_device_ids=true, to_apply=%region_6.7 | all-reduce | flops 8 | bytes 64 | tf_op jit(solution)/shard_map/psum | solution.py:125
  1161.3 0.5 divide_subtract_fusion
  (46 shorter events, 0.6 us)
Async XLA Ops:
  7.2 23.8 %copy-start = (f32[2,8,8,512]{3,2,1,0:T(8,128)S(1)}, f32[2,8,8,512]{3,2,1,0:T(8,128)}, u32[]{:S(2)}) copy-start(f32[2,8,8,512]{3,2,1,0:T(8,128)} %param.13) | copy-start | bytes 786436
  7.2 23.8 %copy-start.1 = (s32[2,8,8,512]{3,2,1,0:T(8,128)S(1)}, s32[2,8,8,512]{3,2,1,0:T(8,128)}, u32[]{:S(2)}) copy-start(s32[2,8,8,512]{3,2,1,0:T(8,128)} %param.14) | copy-start | bytes 786436
  10.6 40.5 %all-to-all-start = ((f32[64,1,512]{2,1,0:T(1,128)}), f32[64,1,512]{2,1,0:T(1,128)S(1)}, u32[]{:S(2)}, u32[]{:S(2)}) async-start(f32[64,1,512]{2,1,0:T(1,128)} %reshape.69), calls=%async_computation | async-start | bytes 262144 | tf_op jit(solution)/shard_map/all_to_all | solution.py:92
  30.9 204.3 %all-reduce.2.cloned.1.call-start = ((), (), s32[]{:S(2)}) async-start(), calls=%async_computation.1 | async-start | bytes 262144 | tf_op jit(solution)/shard_map/psum | solution.py:123
  56.1 2.8 copy-start.4
  59.3 22.6 %collective-permute-start.2 = (f32[8,8,1,512]{3,1,2,0:T(8,128)S(1)}, f32[8,8,1,512]{3,1,2,0:T(8,128)S(1)}, u32[]{:S(2)}, u32[]{:S(2)}) collective-permute-start(f32[8,8,1,512]{3,1,2,0:T(8,128)S(1)} %get-tuple-element.25), channel_id=1, source_target_pairs={{0,2},{2,4},{4,6},{6,8},{8,10},{10,12},{12,14},{14,16},{16,18},{18... | collective-permute-start | bytes 393224 | tf_op jit(solution)/shard_map/ppermute | solution.py:16
  61.8 20.1 %collective-permute-start.3 = (f32[8,8,1,512]{3,1,2,0:T(8,128)S(1)}, f32[8,8,1,512]{3,1,2,0:T(8,128)S(1)}, u32[]{:S(2)}, u32[]{:S(2)}) collective-permute-start(f32[8,8,1,512]{3,1,2,0:T(8,128)S(1)} %get-tuple-element.26), channel_id=1, source_target_pairs={{2,0},{4,2},{6,4},{8,6},{10,8},{12,10},{14,12},{16,14},{18,16},{20... | collective-permute-start | bytes 393224 | tf_op jit(solution)/shard_map/ppermute | solution.py:17
  63.1 11.1 collective-permute-start
  66.1 15.9 %collective-permute-start.1 = (f32[8,8,8,1]{3,1,2,0:T(8,128)S(1)}, f32[8,8,8,1]{3,1,2,0:T(8,128)S(1)}, u32[]{:S(2)}, u32[]{:S(2)}) collective-permute-start(f32[8,8,8,1]{3,1,2,0:T(8,128)S(1)} %get-tuple-element.24), channel_id=1, source_target_pairs={{128,0},{256,128},{384,256},{0,384},{129,1},{257,129},{385,257},{1... | collective-permute-start | bytes 6152 | tf_op jit(solution)/shard_map/ppermute | solution.py:17
  82.7 17.8 %collective-permute-start.6 = (f32[8,8,1,512]{3,1,2,0:T(8,128)S(1)}, f32[8,8,1,512]{3,1,2,0:T(8,128)S(1)}, u32[]{:S(2)}, u32[]{:S(2)}) collective-permute-start(f32[8,8,1,512]{3,1,2,0:T(8,128)S(1)} %get-tuple-element.21), channel_id=1, source_target_pairs={{0,2},{2,4},{4,6},{6,8},{8,10},{10,12},{12,14},{14,16},{16,18},{18... | collective-permute-start | bytes 393224 | tf_op jit(solution)/shard_map/ppermute | solution.py:16
  84.0 17.3 %copy-start.2 = (f32[8,1,1,128]{3,2,1,0:T(1,128)S(1)}, f32[8,1,1,128]{3,2,1,0:T(1,128)}, u32[]{:S(2)}) copy-start(f32[8,1,1,128]{3,2,1,0:T(1,128)} %param.18) | copy-start | bytes 12292
  84.0 17.3 %copy-start.8 = (s32[1,1,128]{2,1,0:T(1,128)S(1)}, s32[1,1,128]{2,1,0:T(1,128)}, u32[]{:S(2)}) copy-start(s32[1,1,128]{2,1,0:T(1,128)} %param.15) | copy-start | bytes 1540
  84.0 16.5 %collective-permute-start.7 = (f32[8,8,1,512]{3,1,2,0:T(8,128)S(1)}, f32[8,8,1,512]{3,1,2,0:T(8,128)S(1)}, u32[]{:S(2)}, u32[]{:S(2)}) collective-permute-start(f32[8,8,1,512]{3,1,2,0:T(8,128)S(1)} %get-tuple-element.22), channel_id=1, source_target_pairs={{2,0},{4,2},{6,4},{8,6},{10,8},{12,10},{14,12},{16,14},{18,16},{20... | collective-permute-start | bytes 393224 | tf_op jit(solution)/shard_map/ppermute | solution.py:17
  85.5 15.0 %collective-permute-start.4 = (f32[8,8,8,1]{3,1,2,0:T(8,128)S(1)}, f32[8,8,8,1]{3,1,2,0:T(8,128)S(1)}, u32[]{:S(2)}, u32[]{:S(2)}) collective-permute-start(f32[8,8,8,1]{3,1,2,0:T(8,128)S(1)} %get-tuple-element.19), channel_id=1, source_target_pairs={{0,128},{128,256},{256,384},{384,0},{1,129},{129,257},{257,385},{3... | collective-permute-start | bytes 6152 | tf_op jit(solution)/shard_map/ppermute | solution.py:16
  91.0 9.6 collective-permute-start.5
  92.9 10.9 copy-start.3
  92.9 13.5 %copy-start.6 = (f32[1,1,128]{2,1,0:T(1,128)S(1)}, f32[1,1,128]{2,1,0:T(1,128)}, u32[]{:S(2)}) copy-start(f32[1,1,128]{2,1,0:T(1,128)} %param.19) | copy-start | bytes 1540
  92.9 13.5 %copy-start.7 = (f32[1,1,128]{2,1,0:T(1,128)S(1)}, f32[1,1,128]{2,1,0:T(1,128)}, u32[]{:S(2)}) copy-start(f32[1,1,128]{2,1,0:T(1,128)} %param.20) | copy-start | bytes 1540
  108.8 23.7 %collective-permute-start.10 = (f32[8,8,1,512]{3,1,2,0:T(8,128)S(1)}, f32[8,8,1,512]{3,1,2,0:T(8,128)S(1)}, u32[]{:S(2)}, u32[]{:S(2)}) collective-permute-start(f32[8,8,1,512]{3,1,2,0:T(8,128)S(1)} %slice.165), channel_id=1, source_target_pairs={{2,0},{4,2},{6,4},{8,6},{10,8},{12,10},{14,12},{16,14},{18,16},{20... | collective-permute-start | bytes 393224 | tf_op jit(solution)/shard_map/ppermute | solution.py:30
  110.1 22.4 %collective-permute-start.11 = (f32[8,8,1,512]{3,1,2,0:T(8,128)S(1)}, f32[8,8,1,512]{3,1,2,0:T(8,128)S(1)}, u32[]{:S(2)}, u32[]{:S(2)}) collective-permute-start(f32[8,8,1,512]{3,1,2,0:T(8,128)S(1)} %slice.166), channel_id=1, source_target_pairs={{0,2},{2,4},{4,6},{6,8},{8,10},{10,12},{12,14},{14,16},{16,18},{18... | collective-permute-start | bytes 393224 | tf_op jit(solution)/shard_map/ppermute | solution.py:30
  115.2 10.7 collective-permute-start.8
  118.4 14.1 %collective-permute-start.9 = (f32[8,8,8,1]{3,1,2,0:T(8,128)S(1)}, f32[8,8,8,1]{3,1,2,0:T(8,128)S(1)}, u32[]{:S(2)}, u32[]{:S(2)}) collective-permute-start(f32[8,8,8,1]{3,1,2,0:T(8,128)S(1)} %slice.162), channel_id=1, source_target_pairs={{0,128},{128,256},{256,384},{384,0},{1,129},{129,257},{257,385},{3... | collective-permute-start | bytes 6152 | tf_op jit(solution)/shard_map/ppermute | solution.py:24
  133.6 16.0 %collective-permute-start.12 = (f32[8,8,8,1]{3,1,2,0:T(8,128)S(1)}, f32[8,8,8,1]{3,1,2,0:T(8,128)S(1)}, u32[]{:S(2)}, u32[]{:S(2)}) collective-permute-start(f32[8,8,8,1]{3,1,2,0:T(8,128)S(1)} %slice.169), channel_id=1, source_target_pairs={{0,384},{128,0},{256,128},{384,256},{1,385},{129,1},{257,129},{385... | collective-permute-start | bytes 6152 | tf_op jit(solution)/shard_map/ppermute | solution.py:24
  138.6 19.1 %collective-permute-start.15 = (f32[8,8,1,512]{3,1,2,0:T(8,128)S(1)}, f32[8,8,1,512]{3,1,2,0:T(8,128)S(1)}, u32[]{:S(2)}, u32[]{:S(2)}) collective-permute-start(f32[8,8,1,512]{3,1,2,0:T(8,128)S(1)} %slice.174), channel_id=1, source_target_pairs={{0,2},{2,4},{4,6},{6,8},{8,10},{10,12},{12,14},{14,16},{16,18},{18... | collective-permute-start | bytes 393224 | tf_op jit(solution)/shard_map/ppermute | solution.py:30
  144.5 22.3 %collective-permute-start.14 = (f32[8,8,1,512]{3,1,2,0:T(8,128)S(1)}, f32[8,8,1,512]{3,1,2,0:T(8,128)S(1)}, u32[]{:S(2)}, u32[]{:S(2)}) collective-permute-start(f32[8,8,1,512]{3,1,2,0:T(8,128)S(1)} %slice.173), channel_id=1, source_target_pairs={{2,0},{4,2},{6,4},{8,6},{10,8},{12,10},{14,12},{16,14},{18,16},{20... | collective-permute-start | bytes 393224 | tf_op jit(solution)/shard_map/ppermute | solution.py:30
  146.0 11.4 collective-permute-start.13
  166.9 68.3 %copy-start.5 = (f32[8]{0:T(128)S(1)}, f32[8]{0:T(128)}, u32[]{:S(2)}) copy-start(f32[8]{0:T(128)} %param.21) | copy-start | bytes 100
Sparse Core Ops, SparseCore 0:
  169.0 66.2 all-reduce.1
where the time goes:
time: 1170 us
  blocking collectives  927 us (79%)
  waiting for transfers between devices  133 us (11%)
  starting transfers between devices  67.6 us (6%)
  between operations  15.2 us (1%)
  local copies, waits for them, and re-layouts  13.2 us (1%)
    psum x1, blocking collectives, on_device(): square_sum = lax.psum(jnp.sum(adj * adj, axis=(1, 2)), ('face', 'tile'))  924 us
    psum x1, waiting for transfers between devices, on_device(): adj = lax.psum(adj_part, 'lev')  66.5 us
  transfers between devices with their start and end apart: 18, of which 9 were waited for; matrix products, arithmetic and copies ran while one was open for 0% of the time, Pallas kernels for 0%

commit v1 on v0

v1 whole, which is shorter than its diff:
```python
import functools

import jax
import jax.numpy as jnp
from jax import lax
from jax.experimental import pallas as pl
from jax.experimental.pallas import tpu as pltpu
from jax.sharding import PartitionSpec as P

KAPPA = 0.025
MESH = pl.DeviceIdType.MESH
F32 = jnp.float32
BF16 = jnp.bfloat16

NT, NLEV, ROWS, COLS, SLOTS = 8, 8, 8, 512, 128
WIDE = COLS + 128
STEPS = ((0, 0), (0, -1), (0, 1), (-1, 0), (1, 0))
OFFSETS = tuple((dy, dx) for dy in range(-2, 3) for dx in range(-2, 3) if abs(dy) + abs(dx) <= 2)
N_OFF = len(OFFSETS)
PLANES = 24


def iota(shape, dim):
    return lax.broadcasted_iota(jnp.int32, shape, dim)


def lroll(x, by):
    by = by % x.shape[-1]
    return x if by == 0 else pltpu.roll(x, by, x.ndim - 1)


def rshift(own, halo, by):
    if by == 0:
        return own, halo
    axis = own.ndim - 2
    turned_own = pltpu.roll(own, by % ROWS, axis)
    turned_halo = pltpu.roll(halo, by % ROWS, axis)
    sub = iota(own.shape, axis)
    cross = sub < by if by > 0 else sub >= ROWS + by
    return jnp.where(cross, turned_halo, turned_own), jnp.where(cross, turned_own, turned_halo)


def exact_dot(values, onehot, dims):
    high = values.astype(BF16)
    rest = values - high.astype(F32)
    middle = rest.astype(BF16)
    low = (rest - middle.astype(F32)).astype(BF16)
    dot = lambda part: lax.dot_general(part, onehot, (dims, ((), ())), preferred_element_type=F32)
    return dot(high) + (dot(middle) + dot(low))


def remote(src, dst, send, recv, device):
    return pltpu.make_async_remote_copy(
        src_ref=src, dst_ref=dst, send_sem=send, recv_sem=recv, device_id=device, device_id_type=MESH
    )


def main_kernel(
    flux_h, cour_h, wind_h, prof, cells, counts, kern, month, observed, obs_w, prec,
    fg_out, sq_out,
    flux_v, cour_v, wind_v, w_own, w_halo, w_edge, col_s, col_r,
    s_buf, i_buf, z_buf, r_buf, h_buf, f_buf,
    l_buf, slot_v, nb, dense, m_sh, a_sh, fg_v, az, ap,
    loc_sem, coef_s, coef_r, st1_s, st1_r, st2_s, st2_r, hal_s, hal_r, fx_s, fx_r,
    lev_s, lev_r, nb_s, nb_r, az_s, az_r, ap_s, ap_r,
):
    face, tile, lev = lax.axis_index("face"), lax.axis_index("tile"), lax.axis_index("lev")
    ty, tz, tx = tile // 16, (tile // 4) % 4, tile % 4
    z, plane = tz * 4 + face, ty * 4 + tx

    def in_plane(k):
        other = lax.rem(plane + k, 16)
        return other, (face, (other // 4) * 16 + tz * 4 + other % 4, lev)

    def in_line(k):
        other = lax.rem(z + k, 16)
        return (other % 4, ty * 16 + (other // 4) * 4 + tx, lev)

    def near(df, dt):
        return (lax.rem(face + 4 + df, 4), lax.rem(tile + 64 + dt, 64), lev)

    peer = (face, tile, 1 - lev)
    sends = ((0, -1), (0, 1), (-1, 0), (1, 0), (-1, -1), (1, -1), (-1, 1), (1, 1))

    bar = pltpu.get_barrier_semaphore()
    greet = [peer] + [in_line(k) for k in range(1, 16)] + [in_plane(k)[1] for k in range(1, 16)]
    greet += [near(*d) for d in sends if d[1] != 0]
    for device in greet:
        pl.semaphore_signal(bar, inc=1, device_id=device, device_id_type=MESH)

    local = [
        pltpu.make_async_copy(flux_h, flux_v, loc_sem.at[0]),
        pltpu.make_async_copy(cour_h, cour_v, loc_sem.at[1]),
        pltpu.make_async_copy(wind_h, wind_v, loc_sem.at[2]),
    ]
    for copy in local:
        copy.start()

    local[0].wait()
    by_tracer = jnp.swapaxes(flux_v[...], 0, 1).reshape(NT * 8, 512)
    turned = jnp.transpose(jnp.concatenate([by_tracer, by_tracer], axis=0)).reshape(64, 8, 128)
    nothing = jnp.zeros((1, 8, 128), F32)
    above = jnp.concatenate([turned[1:], nothing], axis=0)
    below = jnp.concatenate([nothing, turned[:-1]], axis=0)
    around = jnp.where(iota((64, 8, 128), 1) < 4, above, below)
    half = jnp.where(lev == 0, turned, around).reshape(4, 2, 2, 4, 8, 128)
    blocks = jnp.where(iota((4, 2, 4, 8, 128), 4) < 64, half[:, :, 0], half[:, :, 1])
    for y in range(4):
        for x in range(4):
            s_buf[y * 4 + x] = blocks[y, :, x]

    local[1].wait()
    local[2].wait()
    u, v = cour_v[0], cour_v[1]
    east, north = wind_v[0] == 1, wind_v[1] == 1
    w_own[1, :, :, :COLS] = jnp.where(east, 0.0, u) + KAPPA
    w_own[2, :, :, :COLS] = jnp.where(east, u, 0.0) + KAPPA
    w_own[3, :, :, :COLS] = jnp.where(north, 0.0, v) + KAPPA
    w_own[4, :, :, :COLS] = jnp.where(north, v, 0.0) + KAPPA
    w_own[0, :, :, :COLS] = 1.0 - u - v - 4.0 * KAPPA
    lane = iota((ROWS, 128), 1)
    last, first = jnp.zeros((ROWS, 128), F32), jnp.zeros((ROWS, 128), F32)
    for e in range(4):
        for l in range(NLEV):
            k = e * NLEV + l
            last = jnp.where(lane == k, lroll(w_own[1 + e, l, :, COLS - 128 : COLS], k - 127), last)
            first = jnp.where(lane == k, lroll(w_own[1 + e, l, :, :128], k), first)
    col_s[0] = last
    col_s[1] = first

    pl.semaphore_wait(bar, len(greet))

    stage1 = []
    for k in range(1, 16):
        other, device = in_plane(k)
        copy = remote(s_buf.at[other], i_buf.at[plane], st1_s.at[k], st1_r.at[k], device)
        copy.start()
        stage1.append(copy)
    coef = [
        remote(w_own.at[pl.ds(1, 4), :, pl.ds(7, 1), pl.ds(0, COLS)], w_edge.at[:, :, pl.ds(7, 1), :], coef_s.at[0], coef_r.at[0], near(0, 1)),
        remote(w_own.at[pl.ds(1, 4), :, pl.ds(0, 1), pl.ds(0, COLS)], w_edge.at[:, :, pl.ds(0, 1), :], coef_s.at[1], coef_r.at[1], near(0, -1)),
        remote(col_s.at[0], col_r.at[0], coef_s.at[2], coef_r.at[2], near(1, 0)),
        remote(col_s.at[1], col_r.at[1], coef_s.at[3], coef_r.at[3], near(-1, 0)),
    ]
    for copy in coef:
        copy.start()
    i_buf[plane] = s_buf[plane]

    slot = iota((1, SLOTS), 1)
    cell = cells[0].astype(F32)
    row = jnp.floor(cell * (1.0 / COLS))
    col = cell - COLS * row
    sub = iota((ROWS, SLOTS), 0).astype(F32)
    row_mask = jnp.where(sub == row, 1.0, 0.0)
    onehot = jnp.where(iota((COLS, SLOTS), 0).astype(F32) == col, 1.0, 0.0).astype(BF16)
    weight = jnp.where(slot < counts[0, 0], obs_w[0], 0.0)
    kern_rows = (kern[:, 0, 0, :][:, None, :] * row_mask[None]).reshape(NLEV * ROWS, SLOTS)
    kern_dense = exact_dot(kern_rows, onehot, ((1,), (1,))).reshape(NLEV, ROWS, COLS)
    level = iota((NLEV, ROWS, COLS), 0)
    prof_dense = jnp.zeros((NLEV, ROWS, COLS), F32)
    for l in range(NLEV):
        prof_dense = jnp.where(level == l, prof[l], prof_dense)
    kp = kern_dense * prof_dense

    for copy in stage1:
        copy.wait()
    lane6 = iota((2, 4, 8, 128), 3)
    for hi in range(2):
        low_y, high_y = i_buf_view(i_buf, hi)
        z_buf[2 * hi] = jnp.where(lane6 < 64, low_y, lroll(high_y, 64))
        z_buf[2 * hi + 1] = jnp.where(lane6 < 64, lroll(low_y, 64), high_y)
    stage2 = []
    for k in range(1, 4):
        to = lax.rem(tz + k, 4)
        copy = remote(z_buf.at[to], r_buf.at[tz], st2_s.at[k], st2_r.at[k], (face, ty * 16 + to * 4 + tx, lev))
        copy.start()
        stage2.append(copy)

    def halo_copy(side, to):
        there = lax.rem(face + (3 if side == 0 else 1), 4)
        src = (0, 0) if side == 0 else (1, 3)
        device = (there, ty * 16 + to * 4 + tx, lev)
        return remote(z_buf.at[(to, *src)], h_buf.at[side], hal_s.at[side, to], hal_r.at[side], device)

    @pl.when(tz == 0)
    def _():
        for to in range(4):
            halo_copy(0, to).start()

    @pl.when(tz == 3)
    def _():
        for to in range(4):
            halo_copy(1, to).start()

    r_buf[tz] = z_buf[tz]

    for copy in coef:
        copy.wait()
    right, left = col_r[1], col_r[0]
    for e in range(4):
        for l in range(NLEV):
            k = e * NLEV + l
            w_own[1 + e, l, :, COLS:] = jnp.where(
                lane == 0, lroll(right, -k), jnp.where(lane == 127, lroll(left, 127 - k), 0.0)
            )
    w_own[0, :, :, COLS:] = 1.0 - (
        w_own[1, :, :, COLS:] + w_own[2, :, :, COLS:] + w_own[3, :, :, COLS:] + w_own[4, :, :, COLS:]
    )
    sub4 = iota((4, NLEV, ROWS, COLS), 2)
    there = ((sub4 == 0) & (tile < 63)) | ((sub4 == 7) & (tile > 0))
    edges = jnp.where(there, w_edge[...], 0.0)
    w_halo[1:] = edges
    sub3 = iota((NLEV, ROWS, COLS), 1)
    there = ((sub3 == 0) & (tile < 63)) | ((sub3 == 7) & (tile > 0))
    w_halo[0] = jnp.where(there, 1.0 - (edges[0] + edges[1] + edges[2] + edges[3]), 0.0)

    stencil = {}

    def add(offset, term):
        stencil[offset] = stencil[offset] + term if offset in stencil else term

    for e1, (dy, dx) in enumerate(STEPS):
        g = kp * w_own[e1, :, :, :COLS]
        for e2, (ey, ex) in enumerate(STEPS):
            offset = (dy + ey, dx + ex)
            if dy == 0 and dx == 0:
                add(offset, jnp.sum(g * w_own[e2, :, :, :COLS], axis=0))
            elif dy == 0:
                h = lroll(jnp.concatenate([g, jnp.zeros((NLEV, ROWS, 128), F32)], axis=-1), dx)
                add(offset, lroll(jnp.sum(h * w_own[e2], axis=0), -dx)[:, :COLS])
            else:
                h, h_halo = rshift(g, jnp.zeros_like(g), dy)
                p, p_halo = jnp.sum(h * w_own[e2, :, :, :COLS], axis=0), jnp.sum(h_halo * w_halo[e2], axis=0)
                add(offset, rshift(p, p_halo, -dy)[0])
    spread = jnp.concatenate([stencil[o] for o in OFFSETS] + [jnp.zeros((3 * ROWS, COLS), F32)], axis=0)
    picked = exact_dot(spread, onehot, ((1,), (0,))).reshape(16, ROWS, SLOTS)
    l_buf[0] = jnp.sum(picked * row_mask[None], axis=1)
    to_peer = remote(l_buf.at[0], l_buf.at[1], lev_s, lev_r, peer)
    to_peer.start()
    to_peer.wait()

    sub16 = iota((16, SLOTS), 0)
    table = l_buf[0] + l_buf[1]
    table = jnp.where(sub16 == 13, observed[0], table)
    table = jnp.where(sub16 == 14, weight, table)
    slot_v[8:24] = jnp.where(sub16 == 15, cell, table)
    slot_v[0:8] = month[:, 0, 0, :]
    around_copies = []
    for k, d in enumerate(sends):
        copy = remote(slot_v, nb.at[k], nb_s.at[k], nb_r.at[k], near(*d))
        copy.start()
        around_copies.append(copy)

    def rows_of(values, mask):
        return (values[:, None, :] * mask[None]).reshape(PLANES * ROWS, SLOTS)

    own = exact_dot(rows_of(slot_v[...], row_mask), onehot, ((1,), (1,)))
    dense[0, :, :, :COLS] = own.reshape(PLANES, ROWS, COLS)

    for copy in around_copies:
        copy.wait()
    up, down = tile < 63, tile > 0

    def place(k):
        c = nb[k, 23:24, :]
        r = jnp.floor(c * (1.0 / COLS))
        return r, c - COLS * r

    def near_rows(r, upper):
        keep = (r <= 1.0) & up if upper else (r >= 6.0) & down
        return jnp.where((sub == r) & keep, 1.0, 0.0)

    def near_cols(c, righter):
        target = iota((128, SLOTS), 0).astype(F32)
        hit = (target == c) & (c <= 1.0) if righter else (target == c - (COLS - 128.0)) & (c >= COLS - 2.0)
        return jnp.where(hit, 1.0, 0.0).astype(BF16)

    values, hots = [], []
    for k, upper in ((0, True), (1, False)):
        r, c = place(k)
        values.append(rows_of(nb[k], near_rows(r, upper)))
        hots.append(jnp.where(iota((COLS, SLOTS), 0).astype(F32) == c, 1.0, 0.0).astype(BF16))
    out = exact_dot(jnp.concatenate(values, axis=1), jnp.concatenate(hots, axis=1), ((1,), (1,)))
    dense[1, :, :, :COLS] = out.reshape(PLANES, ROWS, COLS)
    values, hots = [], []
    for k, righter in ((2, True), (3, False)):
        r, c = place(k)
        values.append(rows_of(nb[k], jnp.where(sub == r, 1.0, 0.0)))
        hots.append(near_cols(c, righter))
    out = exact_dot(jnp.concatenate(values, axis=1), jnp.concatenate(hots, axis=1), ((1,), (1,)))
    dense[0, :, :, COLS:] = out.reshape(PLANES, ROWS, 128)
    values, hots = [], []
    for k, upper, righter in ((4, True, True), (5, True, False), (6, False, True), (7, False, False)):
        r, c = place(k)
        values.append(rows_of(nb[k], near_rows(r, upper)))
        hots.append(near_cols(c, righter))
    out = exact_dot(jnp.concatenate(values, axis=1), jnp.concatenate(hots, axis=1), ((1,), (1,)))
    dense[1, :, :, COLS:] = out.reshape(PLANES, ROWS, 128)

    for dx in range(-2, 3):
        months = lroll(dense[0, 0:8], dx), lroll(dense[1, 0:8], dx)
        for i, (oy, ox) in enumerate(OFFSETS):
            if ox == dx:
                m_own, m_halo = rshift(*months, oy)
                m_sh[i, 0] = m_own
                m_sh[i, 1] = m_halo
                a_own, a_halo = rshift(lroll(dense[0, 8 + i], dx), lroll(dense[1, 8 + i], dx), oy)
                a_sh[i, 0] = a_own
                a_sh[i, 1] = a_halo

    for copy in stage2:
        copy.wait()

    @pl.when(tz == 0)
    def _():
        for to in range(4):
            halo_copy(0, to).wait_send()

    @pl.when(tz == 3)
    def _():
        for to in range(4):
            halo_copy(1, to).wait_send()

    for side in range(2):
        halo_copy(side, 0).wait_recv()
    parts = [r_buf[i // 4, :, i % 4] for i in range(16)]
    lanes = iota((2, 8, 128), 2)
    for step in (1, 2, 4, 8):
        upper_half = (lanes // (8 * step)) % 2 == 1
        for i in range(16):
            if i & step == 0:
                a, b = parts[i], parts[i + step]
                parts[i] = jnp.where(upper_half, lroll(b, 8 * step), a)
                parts[i + step] = jnp.where(upper_half, b, lroll(a, -8 * step))
    for g in range(16):
        for y in range(2):
            f_buf[lev, g % 8, :, (2 * y + g // 8) * 128 : (2 * y + g // 8 + 1) * 128] = parts[g][y]
    for t in range(NT):
        f_buf[lev, t, :, COLS:] = jnp.where(
            lane < 4, lroll(h_buf[0], -8 * t), jnp.where(lane >= 124, lroll(h_buf[1], 56 - 8 * t), 0.0)
        )
    swap = remote(f_buf.at[lev], f_buf.at[lev], fx_s, fx_r, peer)
    swap.start()
    swap.wait()

    by_row = {}
    for i, (dy, dx) in enumerate(OFFSETS):
        pair = tuple(lroll(a_sh[i, h] * jnp.sum(m_sh[i, h] * f_buf[h], axis=0), -dx) for h in range(2))
        by_row[dy] = tuple(p + q for p, q in zip(by_row[dy], pair)) if dy in by_row else pair
    model = None
    for dy, pair in by_row.items():
        pair = rshift(*pair, -dy)
        model = pair if model is None else tuple(p + q for p, q in zip(model, pair))
    forcing = tuple(dense[h, 22] * (dense[h, 21] - model[h]) for h in range(2))
    adj = jnp.zeros((NT, ROWS, COLS), F32)
    for dx in range(-2, 3):
        moved = tuple(lroll(f, dx) for f in forcing)
        for i, (oy, ox) in enumerate(OFFSETS):
            if ox == dx:
                q = (a_sh[i, 0] * rshift(*moved, oy)[0])[:, :COLS]
                adj = adj + q[None] * m_sh[i, 0, :, :, :COLS]

    square = adj * adj
    square = square[..., :128] + square[..., 128:256] + square[..., 256:384] + square[..., 384:]
    square = jnp.sum(square, axis=1)
    for by in (64, 32, 16):
        square = square + lroll(square, by)
    mine = jnp.where(lane // 16 == iota((ROWS, 128), 0), square, 0.0)
    az[z] = jnp.broadcast_to(jnp.sum(mine, axis=0, keepdims=True), (8, 128))
    copies = []
    for k in range(1, 16):
        copy = remote(az.at[z, pl.ds(0, 1)], az.at[z, pl.ds(0, 1)], az_s.at[k], az_r.at[k], in_line(k))
        copy.start()
        copies.append(copy)
    for t in range(NT):
        fg_v[t] = prec[t] * f_buf[0, t, :, :COLS] - adj[t]
    out_copy = pltpu.make_async_copy(fg_v, fg_out, loc_sem.at[3])
    out_copy.start()
    for copy in copies:
        copy.wait()
    total = az[0, 0:1]
    for i in range(1, 16):
        total = total + az[i, 0:1]
    ap[plane] = jnp.broadcast_to(total, (8, 128))
    copies = []
    for k in range(1, 16):
        copy = remote(ap.at[plane, pl.ds(0, 1)], ap.at[plane, pl.ds(0, 1)], ap_s.at[k], ap_r.at[k], in_plane(k)[1])
        copy.start()
        copies.append(copy)
    for copy in copies:
        copy.wait()
    total = ap[0, 0:1]
    for i in range(1, 16):
        total = total + ap[i, 0:1]
    sq_out[...] = jnp.broadcast_to(total, (8, 128))
    out_copy.wait()


def i_buf_view(i_buf, hi):
    low = jnp.concatenate([i_buf[0:4, hi][None], i_buf[8:12, hi][None]], axis=0)
    high = jnp.concatenate([i_buf[4:8, hi][None], i_buf[12:16, hi][None]], axis=0)
    return low, high


def last_kernel(all_cells, fg_in, sq, prec, fg_out, pg_out, sem):
    copy = pltpu.make_async_copy(fg_in, fg_out, sem)
    copy.start()
    lane, sub = iota((8, 128), 1), iota((8, 128), 0)
    sums = jnp.sum(jnp.where(lane // 16 == sub, sq[...], 0.0), axis=1, keepdims=True)
    row = jnp.sum(jnp.where(lane == sub, sums, 0.0), axis=0, keepdims=True)[:, :8]
    p = prec[...].reshape(1, 8)
    pg_out[...] = (0.5 / p - 0.5 * (row / all_cells) / (p * p)).reshape(8)
    copy.wait()


def on_device(flux, profile, courant, winds, cells, counts, kernels, month_weight, observed, obs_weight, precision):
    vmem = pl.BlockSpec(memory_space=pltpu.VMEM)
    smem = pl.BlockSpec(memory_space=pltpu.SMEM)
    hbm = pl.BlockSpec(memory_space=pl.ANY)
    dma = pltpu.SemaphoreType.DMA

    def buf(*shape, dtype=F32):
        return pltpu.VMEM(shape, dtype)

    fg, sq = pl.pallas_call(
        main_kernel,
        name="gradient",
        out_shape=(jax.ShapeDtypeStruct((NT, ROWS, COLS), F32), jax.ShapeDtypeStruct((8, 128), F32)),
        in_specs=[hbm, hbm, hbm, smem, vmem, smem, vmem, vmem, vmem, vmem, smem],
        out_specs=(hbm, vmem),
        scratch_shapes=[
            buf(8, NT, 512), buf(2, NLEV, ROWS, COLS), buf(2, NLEV, ROWS, COLS, dtype=jnp.int32),
            buf(5, NLEV, ROWS, WIDE), buf(5, NLEV, ROWS, COLS), buf(4, NLEV, ROWS, COLS), buf(2, 8, 128), buf(2, 8, 128),
            buf(16, 2, 8, 128), buf(16, 2, 8, 128), buf(4, 2, 4, 8, 128), buf(4, 2, 4, 8, 128), buf(2, 8, 128),
            buf(2, NT, ROWS, WIDE),
            buf(2, 16, SLOTS), buf(PLANES, SLOTS), buf(8, PLANES, SLOTS), buf(2, PLANES, ROWS, WIDE),
            buf(N_OFF, 2, NT, ROWS, WIDE), buf(N_OFF, 2, ROWS, WIDE), buf(NT, ROWS, COLS), buf(16, 8, 128), buf(16, 8, 128),
            dma((4,)), dma((4,)), dma((4,)), dma((16,)), dma((16,)), dma((4,)), dma((4,)), dma((2, 4)), dma((2,)), dma, dma,
            dma, dma, dma((8,)), dma((8,)), dma((16,)), dma((16,)), dma((16,)), dma((16,)),
        ],
        compiler_params=pltpu.CompilerParams(collective_id=0, has_side_effects=True, vmem_limit_bytes=48 * 2**20),
    )(flux, courant, winds, profile, cells, counts, kernels, month_weight, observed, obs_weight, precision)
    all_cells = float(ROWS * COLS * lax.axis_size("tile") * lax.axis_size("face"))
    return pl.pallas_call(
        functools.partial(last_kernel, all_cells),
        name="finish",
        out_shape=(jax.ShapeDtypeStruct((NT, ROWS, COLS), F32), jax.ShapeDtypeStruct((8,), F32)),
        in_specs=[hbm, vmem, vmem],
        out_specs=(hbm, vmem),
        scratch_shapes=[dma],
    )(fg, sq, precision)


def solution(mesh):
    return jax.shard_map(
        on_device,
        mesh=mesh,
        in_specs=(
            P(("face", "tile"), None, None),
            P("lev"),
            P(None, "lev", "tile", "face"),
            P(None, "lev", "tile", "face"),
            P("tile", "face", None),
            P("tile", "face"),
            P("lev", "tile", "face", None),
            P(None, "tile", "face", None),
            P("tile", "face", None),
            P("tile", "face", None),
            P(),
        ),
        out_specs=(P(None, "tile", "face"), P()),
        check_vma=False,
    )
```

time: 1170 us -> 70.1 us (0.06)
  the two profiles are of different devices: /device:TPU:32 before, /device:TPU:1 now
where the time goes in v1:
time: 70.1 us; the launch traced here: 69.7 us
  Pallas kernels  61.6 us (88%)
  local copies, waits for them, and re-layouts  6.73 us (10%)
  between operations  1.38 us (2%)
    pallas_call x1, Pallas kernels, on_device(): pl.pallas_call(main_kernel, name='gradient', out_shape=(jax.ShapeDtypeStr...  55.4 us
    unnamed x24, local copies, waits for them, and re-layouts  6.73 us
    pallas_call x1, Pallas kernels, on_device(): pl.pallas_call(functools.partial(last_kernel, all_cells), name='finish',...  6.27 us

profile of v1, /device:TPU:1, one launch (start us, length us, event | category | flops | bytes accessed | tf_op | source)
XLA Modules:
  0.0 69.7 jit_solution(5209089898252655672)
XLA Ops:
  0.6 0.0 copy-start.7
  0.6 0.0 copy-start.9
  0.7 0.0 copy-start.8
  1.3 0.0 copy-done.7
  1.3 0.0 copy-done.9
  1.4 0.0 copy-done.8
  1.4 0.0 copy-start
  1.4 0.9 %copy-done = f32[2,8,8,512]{3,2,1,0:T(8,128)S(1)} copy-done((f32[2,8,8,512]{3,2,1,0:T(8,128)S(1)}, f32[2,8,8,512]{3,2,1,0:T(8,128)}, u32[]{:S(2)}) %copy-start) | copy-done | bytes 262168
  2.3 0.0 copy-start.1
  2.3 0.9 %copy-done.1 = s32[2,8,8,512]{3,2,1,0:T(8,128)S(1)} copy-done((s32[2,8,8,512]{3,2,1,0:T(8,128)S(1)}, s32[2,8,8,512]{3,2,1,0:T(8,128)}, u32[]{:S(2)}) %copy-start.1) | copy-done | bytes 262168
  3.3 0.0 copy-start.3
  3.3 0.9 %copy-done.3 = f32[8,8,512]{2,1,0:T(8,128)S(1)} copy-done((f32[8,8,512]{2,1,0:T(8,128)S(1)}, f32[8,8,512]{2,1,0:T(8,128)}, u32[]{:S(2)}) %copy-start.3) | copy-done | bytes 131096
  4.2 0.0 copy-start.4
  4.2 0.7 copy-done.4
  4.9 0.0 copy-start.5
  4.9 0.7 copy-done.5
  5.5 0.0 copy-start.10
  5.5 0.7 copy-done.10
  6.2 0.0 copy-start.11
  6.2 0.7 copy-done.11
  6.9 55.4 %gradient.1 = (f32[8,8,512]{2,1,0:T(8,128)S(1)}, f32[8,128]{1,0:T(8,128)S(1)}) custom-call(f32[8,8,512]{2,1,0:T(8,128)S(1)} %copy-done.3, f32[2,8,8,512]{3,2,1,0:T(8,128)S(1)} %copy-done, s32[2,8,8,512]{3,2,1,0:T(8,128)S(1)} %copy-done.1, f32[8]{0:T(128)S(1)} %copy-done.8, s32[1,1,128]{2,1,0:T(1,128)S(1)} %copy-done.9, s32[1,1]{1,0:T(1,128)S(6)} %copy.13.counts, ...), custom_call_target="tpu_custom_call" | custom-call | tf_op jit(solution)/shard_map/gradient/pallas_call | solution.py:425
  62.2 0.0 copy-start.2
  62.2 0.6 copy-done.2
  62.9 0.0 copy-start.6
  62.9 0.6 copy-done.6
  63.5 6.3 %finish.1 = (f32[8,8,512]{2,1,0:T(8,128)}, f32[8]{0:T(128)}) custom-call(f32[8,8,512]{2,1,0:T(8,128)} %copy-done.2, f32[8,128]{1,0:T(8,128)} %copy-done.6, f32[8]{0:T(128)} %prec.3), custom_call_target="tpu_custom_call" | custom-call | tf_op jit(solution)/shard_map/finish/pallas_call | solution.py:444
Async XLA Ops:
  0.6 0.7 %copy-start.7 = (f32[8]{0:T(128)S(1)}, f32[8]{0:T(128)}, u32[]{:S(2)}) copy-start(f32[8]{0:T(128)} %prec.3) | copy-start | bytes 100
  0.6 0.7 %copy-start.9 = (s32[1,1,128]{2,1,0:T(1,128)S(1)}, s32[1,1,128]{2,1,0:T(1,128)}, u32[]{:S(2)}) copy-start(s32[1,1,128]{2,1,0:T(1,128)} %cells.1) | copy-start | bytes 1540
  0.7 0.7 %copy-start.8 = (f32[8]{0:T(128)S(1)}, f32[8]{0:T(128)}, u32[]{:S(2)}) copy-start(f32[8]{0:T(128)} %prof.1) | copy-start | bytes 100
  1.4 1.0 %copy-start = (f32[2,8,8,512]{3,2,1,0:T(8,128)S(1)}, f32[2,8,8,512]{3,2,1,0:T(8,128)}, u32[]{:S(2)}) copy-start(f32[2,8,8,512]{3,2,1,0:T(8,128)} %cour_h.1) | copy-start | bytes 786436
  2.3 0.9 %copy-start.1 = (s32[2,8,8,512]{3,2,1,0:T(8,128)S(1)}, s32[2,8,8,512]{3,2,1,0:T(8,128)}, u32[]{:S(2)}) copy-start(s32[2,8,8,512]{3,2,1,0:T(8,128)} %wind_h.1) | copy-start | bytes 786436
  3.3 0.9 %copy-start.3 = (f32[8,8,512]{2,1,0:T(8,128)S(1)}, f32[8,8,512]{2,1,0:T(8,128)}, u32[]{:S(2)}) copy-start(f32[8,8,512]{2,1,0:T(8,128)} %flux_h.1) | copy-start | bytes 393220
  4.2 0.7 copy-start.4
  4.9 0.7 copy-start.5
  5.5 0.7 copy-start.10
  6.2 0.7 copy-start.11
  62.2 0.7 copy-start.2
  62.9 0.6 copy-start.6

commit v2 on v1

--- a/solution.py
+++ b/solution.py
@@ -56,11 +56,13 @@
 
 
 def main_kernel(
-    flux_h, cour_h, wind_h, prof, cells, counts, kern, month, observed, obs_w, prec,
-    fg_out, sq_out,
-    flux_v, cour_v, wind_v, w_own, w_halo, w_edge, col_s, col_r,
+    all_cells,
+    flux_h, prof_h, cour_h, wind_h, cells_h, kern_h, month_h, observed_h, obs_w_h, prec_h, counts,
+    fg_out, pg_out,
+    prof, cells, kern, month, observed, obs_w, prec, prec_v,
+    flux_v, cour_v, wind_v, w_own, w_halo, row_s, row_r, col_s, col_r,
     s_buf, i_buf, z_buf, r_buf, h_buf, f_buf,
-    l_buf, slot_v, nb, dense, m_sh, a_sh, fg_v, az, ap,
+    l_buf, slot_v, nb, corner_s, corner_r, dense, m_sh, a_sh, az, ap,
     loc_sem, coef_s, coef_r, st1_s, st1_r, st2_s, st2_r, hal_s, hal_r, fx_s, fx_r,
     lev_s, lev_r, nb_s, nb_r, az_s, az_r, ap_s, ap_r,
 ):
@@ -89,9 +91,13 @@
         pl.semaphore_signal(bar, inc=1, device_id=device, device_id_type=MESH)
 
     local = [
-        pltpu.make_async_copy(flux_h, flux_v, loc_sem.at[0]),
-        pltpu.make_async_copy(cour_h, cour_v, loc_sem.at[1]),
-        pltpu.make_async_copy(wind_h, wind_v, loc_sem.at[2]),
+        pltpu.make_async_copy(src, dst, loc_sem.at[i])
+        for i, (src, dst) in enumerate(
+            (
+                (flux_h, flux_v), (cour_h, cour_v), (wind_h, wind_v), (cells_h, cells), (kern_h, kern),
+                (prof_h, prof), (obs_w_h, obs_w), (observed_h, observed), (month_h, month), (prec_h, prec), (prec_h, prec_v),
+            )
+        )
     ]
     for copy in local:
         copy.start()
@@ -127,25 +133,30 @@
             first = jnp.where(lane == k, lroll(w_own[1 + e, l, :, :128], k), first)
     col_s[0] = last
     col_s[1] = first
+    for e in range(4):
+        row_s[0, e] = w_own[1 + e, :, ROWS - 1, :COLS]
+        row_s[1, e] = w_own[1 + e, :, 0, :COLS]
 
     pl.semaphore_wait(bar, len(greet))
 
+    coef = [
+        remote(row_s.at[0], row_r.at[0], coef_s.at[0], coef_r.at[0], near(0, 1)),
+        remote(row_s.at[1], row_r.at[1], coef_s.at[1], coef_r.at[1], near(0, -1)),
+        remote(col_s.at[0], col_r.at[0], coef_s.at[2], coef_r.at[2], near(1, 0)),
+        remote(col_s.at[1], col_r.at[1], coef_s.at[3], coef_r.at[3], near(-1, 0)),
+    ]
+    for copy in coef:
+        copy.start()
     stage1 = []
     for k in range(1, 16):
         other, device = in_plane(k)
         copy = remote(s_buf.at[other], i_buf.at[plane], st1_s.at[k], st1_r.at[k], device)
         copy.start()
         stage1.append(copy)
-    coef = [
-        remote(w_own.at[pl.ds(1, 4), :, pl.ds(7, 1), pl.ds(0, COLS)], w_edge.at[:, :, pl.ds(7, 1), :], coef_s.at[0], coef_r.at[0], near(0, 1)),
-        remote(w_own.at[pl.ds(1, 4), :, pl.ds(0, 1), pl.ds(0, COLS)], w_edge.at[:, :, pl.ds(0, 1), :], coef_s.at[1], coef_r.at[1], near(0, -1)),
-        remote(col_s.at[0], col_r.at[0], coef_s.at[2], coef_r.at[2], near(1, 0)),
-        remote(col_s.at[1], col_r.at[1], coef_s.at[3], coef_r.at[3], near(-1, 0)),
-    ]
-    for copy in coef:
-        copy.start()
     i_buf[plane] = s_buf[plane]
 
+    for copy in local[3:]:
+        copy.wait()
     slot = iota((1, SLOTS), 1)
     cell = cells[0].astype(F32)
     row = jnp.floor(cell * (1.0 / COLS))
@@ -153,7 +164,7 @@
     sub = iota((ROWS, SLOTS), 0).astype(F32)
     row_mask = jnp.where(sub == row, 1.0, 0.0)
     onehot = jnp.where(iota((COLS, SLOTS), 0).astype(F32) == col, 1.0, 0.0).astype(BF16)
-    weight = jnp.where(slot < counts[0, 0], obs_w[0], 0.0)
+    weight = jnp.where(slot < counts[...], obs_w[0], 0.0)
     kern_rows = (kern[:, 0, 0, :][:, None, :] * row_mask[None]).reshape(NLEV * ROWS, SLOTS)
     kern_dense = exact_dot(kern_rows, onehot, ((1,), (1,))).reshape(NLEV, ROWS, COLS)
     level = iota((NLEV, ROWS, COLS), 0)
@@ -206,13 +217,15 @@
     w_own[0, :, :, COLS:] = 1.0 - (
         w_own[1, :, :, COLS:] + w_own[2, :, :, COLS:] + w_own[3, :, :, COLS:] + w_own[4, :, :, COLS:]
     )
-    sub4 = iota((4, NLEV, ROWS, COLS), 2)
-    there = ((sub4 == 0) & (tile < 63)) | ((sub4 == 7) & (tile > 0))
-    edges = jnp.where(there, w_edge[...], 0.0)
-    w_halo[1:] = edges
-    sub3 = iota((NLEV, ROWS, COLS), 1)
-    there = ((sub3 == 0) & (tile < 63)) | ((sub3 == 7) & (tile > 0))
-    w_halo[0] = jnp.where(there, 1.0 - (edges[0] + edges[1] + edges[2] + edges[3]), 0.0)
+    sub2 = iota((ROWS, COLS), 0)
+    is_up, is_down = (sub2 == 0) & (tile < 63), (sub2 == ROWS - 1) & (tile > 0)
+    for l in range(NLEV):
+        rest = jnp.where(is_up | is_down, 1.0, 0.0)
+        for e in range(4):
+            edge = jnp.where(is_up, row_r[1, e, l : l + 1], jnp.where(is_down, row_r[0, e, l : l + 1], 0.0))
+            w_halo[1 + e, l] = edge
+            rest = rest - edge
+        w_halo[0, l] = rest
 
     stencil = {}
 
@@ -246,8 +259,15 @@
     slot_v[8:24] = jnp.where(sub16 == 15, cell, table)
     slot_v[0:8] = month[:, 0, 0, :]
     around_copies = []
+    every = slot_v[...]
+    lane24, sub24 = iota((PLANES, SLOTS), 1), iota((PLANES, SLOTS), 0)
+    for k, corner in enumerate((0.0, COLS - 1.0, (ROWS - 1.0) * COLS, ROWS * COLS - 1.0)):
+        found = jnp.sum(jnp.where(cell == corner, every, 0.0), axis=1, keepdims=True)
+        line = jnp.sum(jnp.where(lane24 == sub24 + 32 * k, found, 0.0), axis=0, keepdims=True)
+        corner_s[k] = jnp.broadcast_to(line, (8, SLOTS))
     for k, d in enumerate(sends):
-        copy = remote(slot_v, nb.at[k], nb_s.at[k], nb_r.at[k], near(*d))
+        src, dst = (slot_v, nb.at[k]) if k < 4 else (corner_s.at[k - 4, pl.ds(0, 1)], corner_r.at[k - 4, pl.ds(0, 1)])
+        copy = remote(src, dst, nb_s.at[k], nb_r.at[k], near(*d))
         copy.start()
         around_copies.append(copy)
 
@@ -289,12 +309,12 @@
         hots.append(near_cols(c, righter))
     out = exact_dot(jnp.concatenate(values, axis=1), jnp.concatenate(hots, axis=1), ((1,), (1,)))
     dense[0, :, :, COLS:] = out.reshape(PLANES, ROWS, 128)
-    values, hots = [], []
-    for k, upper, righter in ((4, True, True), (5, True, False), (6, False, True), (7, False, False)):
-        r, c = place(k)
-        values.append(rows_of(nb[k], near_rows(r, upper)))
-        hots.append(near_cols(c, righter))
-    out = exact_dot(jnp.concatenate(values, axis=1), jnp.concatenate(hots, axis=1), ((1,), (1,)))
+    corners = corner_r[0, 0:1] + corner_r[1, 0:1] + corner_r[2, 0:1] + corner_r[3, 0:1]
+    corners = jnp.where(lane24 % 32 == sub24, corners, 0.0)
+    mask = jnp.where(((lane < 64) & (sub == 0.0) & up) | ((lane >= 64) & (sub == ROWS - 1.0) & down), 1.0, 0.0)
+    place0, side = iota((128, SLOTS), 0), (iota((128, SLOTS), 1) // 32) % 2
+    hot = jnp.where(place0 == 127 * side, 1.0, 0.0).astype(BF16)
+    out = exact_dot(rows_of(corners, mask), hot, ((1,), (1,)))
     dense[1, :, :, COLS:] = out.reshape(PLANES, ROWS, 128)
 
     for dx in range(-2, 3):
@@ -373,9 +393,7 @@
         copy.start()
         copies.append(copy)
     for t in range(NT):
-        fg_v[t] = prec[t] * f_buf[0, t, :, :COLS] - adj[t]
-    out_copy = pltpu.make_async_copy(fg_v, fg_out, loc_sem.at[3])
-    out_copy.start()
+        fg_out[t] = prec[t] * f_buf[0, t, :, :COLS] - adj[t]
     for copy in copies:
         copy.wait()
     total = az[0, 0:1]
@@ -392,8 +410,10 @@
     total = ap[0, 0:1]
     for i in range(1, 16):
         total = total + ap[i, 0:1]
-    sq_out[...] = jnp.broadcast_to(total, (8, 128))
-    out_copy.wait()
+    sums = jnp.sum(jnp.where(lane // 16 == iota((ROWS, 128), 0), total, 0.0), axis=1, keepdims=True)
+    sums = jnp.sum(jnp.where(lane == iota((ROWS, 128), 0), sums, 0.0), axis=0, keepdims=True)[:, :NT]
+    p = prec_v[...].reshape(1, NT)
+    pg_out[...] = (0.5 / p - 0.5 * (sums / all_cells) / (p * p)).reshape(NT)
 
 
 def i_buf_view(i_buf, hi):
@@ -402,53 +422,46 @@
     return low, high
 
 
-def last_kernel(all_cells, fg_in, sq, prec, fg_out, pg_out, sem):
-    copy = pltpu.make_async_copy(fg_in, fg_out, sem)
-    copy.start()
-    lane, sub = iota((8, 128), 1), iota((8, 128), 0)
-    sums = jnp.sum(jnp.where(lane // 16 == sub, sq[...], 0.0), axis=1, keepdims=True)
-    row = jnp.sum(jnp.where(lane == sub, sums, 0.0), axis=0, keepdims=True)[:, :8]
-    p = prec[...].reshape(1, 8)
-    pg_out[...] = (0.5 / p - 0.5 * (row / all_cells) / (p * p)).reshape(8)
-    copy.wait()
-
-
 def on_device(flux, profile, courant, winds, cells, counts, kernels, month_weight, observed, obs_weight, precision):
     vmem = pl.BlockSpec(memory_space=pltpu.VMEM)
-    smem = pl.BlockSpec(memory_space=pltpu.SMEM)
-    hbm = pl.BlockSpec(memory_space=pl.ANY)
+    hbm = pl.BlockSpec(memory_space=pltpu.HBM)
     dma = pltpu.SemaphoreType.DMA
 
     def buf(*shape, dtype=F32):
         return pltpu.VMEM(shape, dtype)
 
-    fg, sq = pl.pallas_call(
-        main_kernel,
+    def smem(*shape, dtype=F32):
+        return pltpu.SMEM(shape, dtype)
+
+    all_cells = float(ROWS * COLS * lax.axis_size("tile") * lax.axis_size("face"))
+    return pl.pallas_call(
+        functools.partial(main_kernel, all_cells),
         name="gradient",
-        out_shape=(jax.ShapeDtypeStruct((NT, ROWS, COLS), F32), jax.ShapeDtypeStruct((8, 128), F32)),
-        in_specs=[hbm, hbm, hbm, smem, vmem, smem, vmem, vmem, vmem, vmem, smem],
-        out_specs=(hbm, vmem),
+        out_shape=(jax.ShapeDtypeStruct((NT, ROWS, COLS), F32), jax.ShapeDtypeStruct((NT,), F32)),
+        in_specs=[hbm] * 10 + [vmem],
+        out_specs=(vmem, vmem),
         scratch_shapes=[
+            smem(NLEV), buf(1, 1, SLOTS, dtype=jnp.int32), buf(NLEV, 1, 1, SLOTS), buf(NT, 1, 1, SLOTS),
+            buf(1, 1, SLOTS), buf(1, 1, SLOTS), smem(NT), buf(NT),
             buf(8, NT, 512), buf(2, NLEV, ROWS, COLS), buf(2, NLEV, ROWS, COLS, dtype=jnp.int32),
-            buf(5, NLEV, ROWS, WIDE), buf(5, NLEV, ROWS, COLS), buf(4, NLEV, ROWS, COLS), buf(2, 8, 128), buf(2, 8, 128),
+            buf(5, NLEV, ROWS, WIDE), buf(5, NLEV, ROWS, COLS), buf(2, 4, NLEV, COLS), buf(2, 4, NLEV, COLS),
+            buf(2, 8, 128), buf(2, 8, 128),
             buf(16, 2, 8, 128), buf(16, 2, 8, 128), buf(4, 2, 4, 8, 128), buf(4, 2, 4, 8, 128), buf(2, 8, 128),
             buf(2, NT, ROWS, WIDE),
-            buf(2, 16, SLOTS), buf(PLANES, SLOTS), buf(8, PLANES, SLOTS), buf(2, PLANES, ROWS, WIDE),
-            buf(N_OFF, 2, NT, ROWS, WIDE), buf(N_OFF, 2, ROWS, WIDE), buf(NT, ROWS, COLS), buf(16, 8, 128), buf(16, 8, 128),
-            dma((4,)), dma((4,)), dma((4,)), dma((16,)), dma((16,)), dma((4,)), dma((4,)), dma((2, 4)), dma((2,)), dma, dma,
+            buf(2, 16, SLOTS), buf(PLANES, SLOTS), buf(4, PLANES, SLOTS), buf(4, 8, SLOTS), buf(4, 8, SLOTS),
+            buf(2, PLANES, ROWS, WIDE),
+            buf(N_OFF, 2, NT, ROWS, WIDE), buf(N_OFF, 2, ROWS, WIDE), buf(16, 8, 128), buf(16, 8, 128),
+            dma((11,)), dma((4,)), dma((4,)), dma((16,)), dma((16,)), dma((4,)), dma((4,)), dma((2, 4)), dma((2,)), dma, dma,
             dma, dma, dma((8,)), dma((8,)), dma((16,)), dma((16,)), dma((16,)), dma((16,)),
         ],
-        compiler_params=pltpu.CompilerParams(collective_id=0, has_side_effects=True, vmem_limit_bytes=48 * 2**20),
-    )(flux, courant, winds, profile, cells, counts, kernels, month_weight, observed, obs_weight, precision)
-    all_cells = float(ROWS * COLS * lax.axis_size("tile") * lax.axis_size("face"))
-    return pl.pallas_call(
-        functools.partial(last_kernel, all_cells),
-        name="finish",
-        out_shape=(jax.ShapeDtypeStruct((NT, ROWS, COLS), F32), jax.ShapeDtypeStruct((8,), F32)),
-        in_specs=[hbm, vmem, vmem],
-        out_specs=(hbm, vmem),
-        scratch_shapes=[dma],
-    )(fg, sq, precision)
+        compiler_params=pltpu.CompilerParams(collective_id=0, has_side_effects=True, vmem_limit_bytes=40 * 2**20),
+    )(
+        *(
+            pltpu.with_memory_space_constraint(x, pltpu.HBM)
+            for x in (flux, profile, courant, winds, cells, kernels, month_weight, observed, obs_weight, precision)
+        ),
+        jnp.broadcast_to(counts, (1, SLOTS)),
+    )
 
 
 def solution(mesh):

time: 70.1 us -> 54.7 us (0.78)
  Pallas kernels: 61.6 us -> 52 us
  local copies, waits for them, and re-layouts: 6.73 us -> 1.17 us
    pallas_call x2 -> x1, Pallas kernels: 61.6 us -> 52 us  [on_device(): pl.pallas_call(functools.partial(main_kernel, all_cells), name='gradient'...]
    unnamed x24 -> x2, local copies, waits for them, and re-layouts: 6.73 us -> 1.17 us
where the time goes in v2:
time: 54.7 us; the launch traced here: 54.5 us
  Pallas kernels  52 us (95%)
  between operations  1.29 us (2%)
  local copies, waits for them, and re-layouts  1.17 us (2%)
    pallas_call x1, Pallas kernels, on_device(): pl.pallas_call(functools.partial(main_kernel, all_cells), name='gradient'...  52 us
    unnamed x2, local copies, waits for them, and re-layouts  1.17 us

profile of v2, /device:TPU:1, one launch (start us, length us, event | category | flops | bytes accessed | tf_op | source)
XLA Modules:
  0.0 54.5 jit_solution(15908991222471965238)
XLA Ops:
  1.3 52.0 %gradient.1 = (f32[8,8,512]{2,1,0:T(8,128)S(1)}, f32[8]{0:T(128)S(1)}) custom-call(f32[8,8,512]{2,1,0:T(8,128)} %flux_h.1, f32[8]{0:T(128)} %prof_h.1, f32[2,8,8,512]{3,2,1,0:T(8,128)} %cour_h.1, s32[2,8,8,512]{3,2,1,0:T(8,128)} %wind_h.1, s32[1,1,128]{2,1,0:T(1,128)} %cells_h.1, f32[8,1,1,128]{3,2,1,0:T(1,128)} %kern_h.1, f32[8,1,1,128]{3,2,1,0:T(1,128)} %month_h.1, ...), custom_call_target="tpu_custom_call" | custom-call | tf_op jit(solution)/shard_map/gradient/pallas_call | solution.py:437
  53.3 0.7 %copy.16 = f32[8,8,512]{2,1,0:T(8,128)} copy(f32[8,8,512]{2,1,0:T(8,128)S(1)} %get-tuple-element.4) | data formatting | bytes 262144
  54.0 0.5 copy.17
  (1 shorter events, 0.0 us)

commit v3 on v2

--- a/solution.py
+++ b/solution.py
@@ -277,6 +277,40 @@
     own = exact_dot(rows_of(slot_v[...], row_mask), onehot, ((1,), (1,)))
     dense[0, :, :, :COLS] = own.reshape(PLANES, ROWS, COLS)
 
+    for copy in stage2:
+        copy.wait()
+
+    @pl.when(tz == 0)
+    def _():
+        for to in range(4):
+            halo_copy(0, to).wait_send()
+
+    @pl.when(tz == 3)
+    def _():
+        for to in range(4):
+            halo_copy(1, to).wait_send()
+
+    for side in range(2):
+        halo_copy(side, 0).wait_recv()
+    parts = [r_buf[i // 4, :, i % 4] for i in range(16)]
+    lanes = iota((2, 8, 128), 2)
+    for step in (1, 2, 4, 8):
+        upper_half = (lanes // (8 * step)) % 2 == 1
+        for i in range(16):
+            if i & step == 0:
+                a, b = parts[i], parts[i + step]
+                parts[i] = jnp.where(upper_half, lroll(b, 8 * step), a)
+                parts[i + step] = jnp.where(upper_half, b, lroll(a, -8 * step))
+    for g in range(16):
+        for y in range(2):
+            f_buf[lev, g % 8, :, (2 * y + g // 8) * 128 : (2 * y + g // 8 + 1) * 128] = parts[g][y]
+    for t in range(NT):
+        f_buf[lev, t, :, COLS:] = jnp.where(
+            lane < 4, lroll(h_buf[0], -8 * t), jnp.where(lane >= 124, lroll(h_buf[1], 56 - 8 * t), 0.0)
+        )
+    swap = remote(f_buf.at[lev], f_buf.at[lev], fx_s, fx_r, peer)
+    swap.start()
+
     for copy in around_copies:
         copy.wait()
     up, down = tile < 63, tile > 0
@@ -328,39 +362,6 @@
                 a_sh[i, 0] = a_own
                 a_sh[i, 1] = a_halo
 
-    for copy in stage2:
-        copy.wait()
-
-    @pl.when(tz == 0)
-    def _():
-        for to in range(4):
-            halo_copy(0, to).wait_send()
-
-    @pl.when(tz == 3)
-    def _():
-        for to in range(4):
-            halo_copy(1, to).wait_send()
-
-    for side in range(2):
-        halo_copy(side, 0).wait_recv()
-    parts = [r_buf[i // 4, :, i % 4] for i in range(16)]
-    lanes = iota((2, 8, 128), 2)
-    for step in (1, 2, 4, 8):
-        upper_half = (lanes // (8 * step)) % 2 == 1
-        for i in range(16):
-            if i & step == 0:
-                a, b = parts[i], parts[i + step]
-                parts[i] = jnp.where(upper_half, lroll(b, 8 * step), a)
-                parts[i + step] = jnp.where(upper_half, b, lroll(a, -8 * step))
-    for g in range(16):
-        for y in range(2):
-            f_buf[lev, g % 8, :, (2 * y + g // 8) * 128 : (2 * y + g // 8 + 1) * 128] = parts[g][y]
-    for t in range(NT):
-        f_buf[lev, t, :, COLS:] = jnp.where(
-            lane < 4, lroll(h_buf[0], -8 * t), jnp.where(lane >= 124, lroll(h_buf[1], 56 - 8 * t), 0.0)
-        )
-    swap = remote(f_buf.at[lev], f_buf.at[lev], fx_s, fx_r, peer)
-    swap.start()
     swap.wait()
 
     by_row = {}

time: 54.7 us -> 53.2 us (0.973); the launches traced: 54.5 us -> 52.4 us
  Pallas kernels: 52 us -> 50 us
    pallas_call x1, Pallas kernels: 52 us -> 50 us  [on_device(): pl.pallas_call(functools.partial(main_kernel, all_cells), name='gradient'...]
where the time goes in v3:
time: 53.2 us; the launch traced here: 52.4 us
  Pallas kernels  50 us (94%)
  between operations  1.29 us (2%)
  local copies, waits for them, and re-layouts  1.17 us (2%)
    pallas_call x1, Pallas kernels, on_device(): pl.pallas_call(functools.partial(main_kernel, all_cells), name='gradient'...  50 us
    unnamed x2, local copies, waits for them, and re-layouts  1.17 us

profile of v3, /device:TPU:1, one launch (start us, length us, event | category | flops | bytes accessed | tf_op | source)
XLA Modules:
  0.0 52.4 jit_solution(4118217990980304581)
XLA Ops:
  1.3 50.0 %gradient.1 = (f32[8,8,512]{2,1,0:T(8,128)S(1)}, f32[8]{0:T(128)S(1)}) custom-call(f32[8,8,512]{2,1,0:T(8,128)} %flux_h.1, f32[8]{0:T(128)} %prof_h.1, f32[2,8,8,512]{3,2,1,0:T(8,128)} %cour_h.1, s32[2,8,8,512]{3,2,1,0:T(8,128)} %wind_h.1, s32[1,1,128]{2,1,0:T(1,128)} %cells_h.1, f32[8,1,1,128]{3,2,1,0:T(1,128)} %kern_h.1, f32[8,1,1,128]{3,2,1,0:T(1,128)} %month_h.1, ...), custom_call_target="tpu_custom_call" | custom-call | tf_op jit(solution)/shard_map/gradient/pallas_call | solution.py:438
  51.3 0.7 %copy.16 = f32[8,8,512]{2,1,0:T(8,128)} copy(f32[8,8,512]{2,1,0:T(8,128)S(1)} %get-tuple-element.4) | data formatting | bytes 262144
  51.9 0.5 copy.17
  (1 shorter events, 0.0 us)

commit v4 on v3

--- a/solution.py
+++ b/solution.py
@@ -14,6 +14,7 @@
 
 NT, NLEV, ROWS, COLS, SLOTS = 8, 8, 8, 512, 128
 WIDE = COLS + 128
+FAR_FIRST = tuple(sorted(range(1, 16), key=lambda k: -min(k, 16 - k)))
 STEPS = ((0, 0), (0, -1), (0, 1), (-1, 0), (1, 0))
 OFFSETS = tuple((dy, dx) for dy in range(-2, 3) for dx in range(-2, 3) if abs(dy) + abs(dx) <= 2)
 N_OFF = len(OFFSETS)
@@ -64,7 +65,7 @@
     s_buf, i_buf, z_buf, r_buf, h_buf, f_buf,
     l_buf, slot_v, nb, corner_s, corner_r, dense, m_sh, a_sh, az, ap,
     loc_sem, coef_s, coef_r, st1_s, st1_r, st2_s, st2_r, hal_s, hal_r, fx_s, fx_r,
-    lev_s, lev_r, nb_s, nb_r, az_s, az_r, ap_s, ap_r,
+    lev_s, lev_r, nb_s, nb_r, corner_ss, corner_sr, az_s, az_r, ap_s, ap_r,
 ):
     face, tile, lev = lax.axis_index("face"), lax.axis_index("tile"), lax.axis_index("lev")
     ty, tz, tx = tile // 16, (tile // 4) % 4, tile % 4
@@ -78,15 +79,16 @@
         other = lax.rem(z + k, 16)
         return (other % 4, ty * 16 + (other // 4) * 4 + tx, lev)
 
-    def near(df, dt):
-        return (lax.rem(face + 4 + df, 4), lax.rem(tile + 64 + dt, 64), lev)
+    def near(df, dt, core=lev):
+        return (lax.rem(face + 4 + df, 4), lax.rem(tile + 64 + dt, 64), core)
 
     peer = (face, tile, 1 - lev)
     sends = ((0, -1), (0, 1), (-1, 0), (1, 0), (-1, -1), (1, -1), (-1, 1), (1, 1))
 
     bar = pltpu.get_barrier_semaphore()
-    greet = [peer] + [in_line(k) for k in range(1, 16)] + [in_plane(k)[1] for k in range(1, 16)]
-    greet += [near(*d) for d in sends if d[1] != 0]
+    greet = [near(*d, core) for d in sends[4:] for core in (lev, 1 - lev)]
+    greet += [in_line(k) for k in FAR_FIRST] + [near(*d) for d in sends[:2]]
+    greet += [in_plane(k)[1] for k in range(1, 16)] + [peer]
     for device in greet:
         pl.semaphore_signal(bar, inc=1, device_id=device, device_id_type=MESH)
 
@@ -250,24 +252,33 @@
     l_buf[0] = jnp.sum(picked * row_mask[None], axis=1)
     to_peer = remote(l_buf.at[0], l_buf.at[1], lev_s, lev_r, peer)
     to_peer.start()
+
+    sub16 = iota((16, SLOTS), 0)
+    core0 = lev == 0
+    part = jnp.where(sub16 == 13, jnp.where(core0, observed[0], 0.0), l_buf[0])
+    part = jnp.where(sub16 == 14, jnp.where(core0, weight, 0.0), part)
+    every = jnp.concatenate([jnp.where(core0, month[:, 0, 0, :], 0.0), part], axis=0)
+    lane24, sub24 = iota((PLANES, SLOTS), 1), iota((PLANES, SLOTS), 0)
+    corner_copies = []
+    for k, corner in enumerate((0.0, COLS - 1.0, (ROWS - 1.0) * COLS, ROWS * COLS - 1.0)):
+        found = jnp.sum(jnp.where(cell == corner, every, 0.0), axis=1, keepdims=True)
+        line = jnp.sum(jnp.where(lane24 == sub24 + 32 * k, found, 0.0), axis=0, keepdims=True)
+        corner_s[k] = jnp.broadcast_to(line, (8, SLOTS))
+        for i, core in enumerate((lev, 1 - lev)):
+            src, dst = corner_s.at[k, pl.ds(0, 1)], corner_r.at[2 * k + lev, pl.ds(0, 1)]
+            copy = remote(src, dst, corner_ss.at[2 * k + i], corner_sr.at[2 * k + lev], near(*sends[4 + k], core))
+            copy.start()
+            corner_copies.append(copy)
     to_peer.wait()
 
-    sub16 = iota((16, SLOTS), 0)
     table = l_buf[0] + l_buf[1]
     table = jnp.where(sub16 == 13, observed[0], table)
     table = jnp.where(sub16 == 14, weight, table)
     slot_v[8:24] = jnp.where(sub16 == 15, cell, table)
     slot_v[0:8] = month[:, 0, 0, :]
     around_copies = []
-    every = slot_v[...]
-    lane24, sub24 = iota((PLANES, SLOTS), 1), iota((PLANES, SLOTS), 0)
-    for k, corner in enumerate((0.0, COLS - 1.0, (ROWS - 1.0) * COLS, ROWS * COLS - 1.0)):
-        found = jnp.sum(jnp.where(cell == corner, every, 0.0), axis=1, keepdims=True)
-        line = jnp.sum(jnp.where(lane24 == sub24 + 32 * k, found, 0.0), axis=0, keepdims=True)
-        corner_s[k] = jnp.broadcast_to(line, (8, SLOTS))
-    for k, d in enumerate(sends):
-        src, dst = (slot_v, nb.at[k]) if k < 4 else (corner_s.at[k - 4, pl.ds(0, 1)], corner_r.at[k - 4, pl.ds(0, 1)])
-        copy = remote(src, dst, nb_s.at[k], nb_r.at[k], near(*d))
+    for k, d in enumerate(sends[:4]):
+        copy = remote(slot_v, nb.at[k], nb_s.at[k], nb_r.at[k], near(*d))
         copy.start()
         around_copies.append(copy)
 
@@ -313,6 +324,11 @@
 
     for copy in around_copies:
         copy.wait()
+    for copy in corner_copies:
+        copy.wait_send()
+    for i in range(8):
+        row = corner_r.at[i, pl.ds(0, 1)]
+        remote(row, row, corner_ss.at[i], corner_sr.at[i], near(*sends[4 + i // 2])).wait_recv()
     up, down = tile < 63, tile > 0
 
     def place(k):
@@ -343,7 +359,9 @@
         hots.append(near_cols(c, righter))
     out = exact_dot(jnp.concatenate(values, axis=1), jnp.concatenate(hots, axis=1), ((1,), (1,)))
     dense[0, :, :, COLS:] = out.reshape(PLANES, ROWS, 128)
-    corners = corner_r[0, 0:1] + corner_r[1, 0:1] + corner_r[2, 0:1] + corner_r[3, 0:1]
+    corners = corner_r[0, 0:1]
+    for i in range(1, 8):
+        corners = corners + corner_r[i, 0:1]
     corners = jnp.where(lane24 % 32 == sub24, corners, 0.0)
     mask = jnp.where(((lane < 64) & (sub == 0.0) & up) | ((lane >= 64) & (sub == ROWS - 1.0) & down), 1.0, 0.0)
     place0, side = iota((128, SLOTS), 0), (iota((128, SLOTS), 1) // 32) % 2
@@ -389,7 +407,7 @@
     mine = jnp.where(lane // 16 == iota((ROWS, 128), 0), square, 0.0)
     az[z] = jnp.broadcast_to(jnp.sum(mine, axis=0, keepdims=True), (8, 128))
     copies = []
-    for k in range(1, 16):
+    for k in FAR_FIRST:
         copy = remote(az.at[z, pl.ds(0, 1)], az.at[z, pl.ds(0, 1)], az_s.at[k], az_r.at[k], in_line(k))
         copy.start()
         copies.append(copy)
@@ -449,11 +467,11 @@
             buf(2, 8, 128), buf(2, 8, 128),
             buf(16, 2, 8, 128), buf(16, 2, 8, 128), buf(4, 2, 4, 8, 128), buf(4, 2, 4, 8, 128), buf(2, 8, 128),
             buf(2, NT, ROWS, WIDE),
-            buf(2, 16, SLOTS), buf(PLANES, SLOTS), buf(4, PLANES, SLOTS), buf(4, 8, SLOTS), buf(4, 8, SLOTS),
+            buf(2, 16, SLOTS), buf(PLANES, SLOTS), buf(4, PLANES, SLOTS), buf(4, 8, SLOTS), buf(8, 8, SLOTS),
             buf(2, PLANES, ROWS, WIDE),
             buf(N_OFF, 2, NT, ROWS, WIDE), buf(N_OFF, 2, ROWS, WIDE), buf(16, 8, 128), buf(16, 8, 128),
             dma((11,)), dma((4,)), dma((4,)), dma((16,)), dma((16,)), dma((4,)), dma((4,)), dma((2, 4)), dma((2,)), dma, dma,
-            dma, dma, dma((8,)), dma((8,)), dma((16,)), dma((16,)), dma((16,)), dma((16,)),
+            dma, dma, dma((4,)), dma((4,)), dma((8,)), dma((8,)), dma((16,)), dma((16,)), dma((16,)), dma((16,)),
         ],
         compiler_params=pltpu.CompilerParams(collective_id=0, has_side_effects=True, vmem_limit_bytes=40 * 2**20),
     )(

time: 53.2 us -> 52.8 us (level); the launches traced: 52.4 us -> 52.6 us
  no operation moved by 1% of the time
where the time goes in v4:
time: 52.8 us; the launch traced here: 52.6 us
  Pallas kernels  50.1 us (95%)
  between operations  1.29 us (2%)
  local copies, waits for them, and re-layouts  1.17 us (2%)
    pallas_call x1, Pallas kernels, on_device(): pl.pallas_call(functools.partial(main_kernel, all_cells), name='gradient'...  50.1 us
    unnamed x2, local copies, waits for them, and re-layouts  1.17 us

profile of v4, /device:TPU:1, one launch (start us, length us, event | category | flops | bytes accessed | tf_op | source)
XLA Modules:
  0.0 52.6 jit_solution(645636989019595421)
XLA Ops:
  1.3 50.1 %gradient.1 = (f32[8,8,512]{2,1,0:T(8,128)S(1)}, f32[8]{0:T(128)S(1)}) custom-call(f32[8,8,512]{2,1,0:T(8,128)} %flux_h.1, f32[8]{0:T(128)} %prof_h.1, f32[2,8,8,512]{3,2,1,0:T(8,128)} %cour_h.1, s32[2,8,8,512]{3,2,1,0:T(8,128)} %wind_h.1, s32[1,1,128]{2,1,0:T(1,128)} %cells_h.1, f32[8,1,1,128]{3,2,1,0:T(1,128)} %kern_h.1, f32[8,1,1,128]{3,2,1,0:T(1,128)} %month_h.1, ...), custom_call_target="tpu_custom_call" | custom-call | tf_op jit(solution)/shard_map/gradient/pallas_call | solution.py:456
  51.4 0.7 %copy.16 = f32[8,8,512]{2,1,0:T(8,128)} copy(f32[8,8,512]{2,1,0:T(8,128)S(1)} %get-tuple-element.4) | data formatting | bytes 262144
  52.1 0.5 copy.17
  (1 shorter events, 0.0 us)
